TPU v7x, 32 devices: a whole 2x2x4 slice. The times are simulated.
32 devices in a mesh: groups: 2 (over y), tiles: 16 (over z, x, core).
Axes of the slice: x: 2, y: 2, z: 4, core: 2. Of those that a mesh axis runs over, the one named last changes fastest.
Arguments:
- ocean_state: float32 [3, 4, 256, 4352], P(None, 'groups', 'tiles'), parts along dimension 1, may hold values from -6 to 6
- ice_dynamics: float32 [32, 10, 128, 128], P('tiles', 'groups'), parts along dimension 1, may hold values from -3 to 3
- ice_thickness: float32 [32, 10, 128, 128], P('tiles', 'groups'), parts along dimension 1, may hold values from 0.2 to 1
- ice_table: int32 [32, 2], P('groups'), parts along dimension 0, may hold values from -1 to 67, as said below
- land_mask: int32 [136], P('groups'), parts along dimension 0, may hold values from 0 to 1, as said below
Outputs:
- ocean_next: float32 [3, 4, 256, 4352], P(None, 'groups', 'tiles'), parts along dimension 1
- ice_next: float32 [32, 10, 128, 128], P('tiles', 'groups'), parts along dimension 1
There are 2 independent parts, one for each index of `groups`. A program takes and returns all parts, laid end to end along the dimension named above; each array names one. Nothing has to cross between parts.
Inputs may be any that keep to these rules, and one draw needn't show every extreme that they name: `ice_table`: entries are block ids or -1; filled entries are distinct blocks that are not land; an owner's filled slots come first and lie in different rows of blocks; at least a quarter of the owners fill all 2 slots and one owner holds none. `land_mask`: every row of blocks has at least as many blocks that are not land as ice_table places in it.
All inputs are finite; a program needn't handle non-finite values.
Results may differ from a plain program's by a relative error of at most 0.000078.
Values sent between devices are 32-bit elements; how exact they have to be, the bound alone decides.
A program may use at most 64 MiB of HBM per device.

v0:
```python
import jax
import jax.numpy as jnp
from jax import lax
from jax.sharding import PartitionSpec as P

BLK = 128
NSUB = 8


TIME_STEP = 0.1
MIX_HORIZ = 0.5
MIX_VERT = 0.25
CORIOLIS = 0.5
STRESS_GAIN = 2.0
RELAXATION = 0.2
ICE_STEP = 0.5
DRAG_COEFF = 1.0
ECC_SQUARED = 4.0
DELTA_FLOOR = 0.25
STRENGTH_SCALE = 0.25
HEAT_RATE = 0.5
FREEZING = -1.0
CATEGORY_WEIGHTS = (0.5, 0.75, 1.0, 1.25, 1.5)


def padded_2(cells, sides, width):
    for axis, dim in sides:
        count = lax.axis_size(axis)
        ends = count - 1
        head = lax.slice_in_dim(cells, 0, width, axis=dim)
        tail = lax.slice_in_dim(cells, cells.shape[dim] - width, cells.shape[dim], axis=dim)
        cells = jnp.concatenate(
            [
                lax.ppermute(tail, axis, [(i, (i + 1) % count) for i in range(ends)]),
                cells,
                lax.ppermute(head, axis, [((i + 1) % count, i) for i in range(ends)]),
            ],
            axis=dim,
        )
    return cells


def slope_east(values):
    widths = [(0, 0)] * (values.ndim - 1) + [(1, 1)]
    padded = jnp.pad(values, widths)
    return 0.5 * (padded[..., 2:] - padded[..., :-2])


def slope_north(values):
    widths = [(0, 0)] * (values.ndim - 2) + [(1, 1), (0, 0)]
    padded = jnp.pad(values, widths)
    return 0.5 * (padded[..., 2:, :] - padded[..., :-2, :])


def ice_block(currents, thickness, dynamics):
    ocean_u = currents[0]
    ocean_v = currents[1]
    weights = jnp.asarray(CATEGORY_WEIGHTS, dtype=thickness.dtype).reshape(-1, 1, 1)
    total_thick = jnp.sum(thickness, axis=0)
    strength = STRENGTH_SCALE * jnp.sum(weights * thickness, axis=0)
    ice_cover = 1.0 - jnp.exp(-total_thick)
    inertia = total_thick / ICE_STEP
    ice_u = dynamics[0]
    ice_v = dynamics[1]
    stress_sum = dynamics[2]
    stress_diff = dynamics[3]
    stress_shear = dynamics[4]
    for substep in range(NSUB):
        east_u = slope_east(ice_u)
        north_v = slope_north(ice_v)
        north_u = slope_north(ice_u)
        east_v = slope_east(ice_v)
        divergence = east_u + north_v
        tension = east_u - north_v
        shearing = north_u + east_v
        delta_norm = jnp.sqrt(
            divergence * divergence
            + (tension * tension + shearing * shearing) / ECC_SQUARED
            + DELTA_FLOOR
        )
        bulk_viscosity = strength / (2.0 * delta_norm)
        shear_viscosity = bulk_viscosity / ECC_SQUARED
        stress_sum = (1.0 - RELAXATION) * stress_sum + RELAXATION * (
            bulk_viscosity * divergence - 0.5 * strength
        )
        stress_diff = (1.0 - RELAXATION) * stress_diff + RELAXATION * (shear_viscosity * tension)
        stress_shear = (1.0 - RELAXATION) * stress_shear + RELAXATION * (shear_viscosity * shearing)
        force_x = 0.5 * (slope_east(stress_sum) + slope_east(stress_diff)) + slope_north(
            stress_shear
        )
        force_y = 0.5 * (slope_north(stress_sum) - slope_north(stress_diff)) + slope_east(
            stress_shear
        )
        relative_u = ocean_u - ice_u
        relative_v = ocean_v - ice_v
        water_drag = DRAG_COEFF * jnp.sqrt(
            relative_u * relative_u + relative_v * relative_v + 0.0001
        )
        denominator = inertia + water_drag
        next_u = (
            inertia * ice_u + force_x + water_drag * ocean_u + CORIOLIS * total_thick * ice_v
        ) / denominator
        next_v = (
            inertia * ice_v + force_y + water_drag * ocean_v - CORIOLIS * total_thick * ice_u
        ) / denominator
        ice_u = next_u
        ice_v = next_v
    relative_u = ocean_u - ice_u
    relative_v = ocean_v - ice_v
    water_drag = DRAG_COEFF * jnp.sqrt(relative_u * relative_u + relative_v * relative_v + 0.0001)
    stress_x = water_drag * (ice_u - ocean_u)
    stress_y = water_drag * (ice_v - ocean_v)
    dynamics_next = jnp.stack([ice_u, ice_v, stress_sum, stress_diff, stress_shear])
    return (dynamics_next, stress_x, stress_y, ice_cover)


def tendency(padded):
    centre = padded[:, :, 1:-1, :]
    upper_rows = padded[:, :, 2:, :]
    lower_rows = padded[:, :, :-2, :]
    east_cells = jnp.roll(centre, -1, axis=3)
    west_cells = jnp.roll(centre, 1, axis=3)
    laplace = upper_rows + lower_rows + east_cells + west_cells - 4.0 * centre
    grad_x = 0.5 * (east_cells - west_cells)
    grad_y = 0.5 * (upper_rows - lower_rows)
    advection = centre[1] * grad_x + centre[2] * grad_y
    zero_level = jnp.zeros_like(centre[:, :1])
    upward_diff = jnp.concatenate([centre[:, 1:] - centre[:, :-1], zero_level], axis=1)
    downward_diff = jnp.concatenate([zero_level, centre[:, :-1] - centre[:, 1:]], axis=1)
    rotation = CORIOLIS * jnp.stack([jnp.zeros_like(centre[0]), centre[2], -centre[1]])
    return MIX_HORIZ * laplace - advection + MIX_VERT * (upward_diff + downward_diff) + rotation


def shards(ocean_state, ice_dynamics, ice_thickness, ice_table, land_mask):
    device = lax.axis_index("tiles")
    owners = lax.axis_size("tiles")
    band_rows = ocean_state.shape[2]
    band_width = ocean_state.shape[3]
    columns = band_width // BLK
    sources = BLK // band_rows
    slot_count = ice_dynamics.shape[0]
    padded = padded_2(ocean_state, (("tiles", 2),), 1)
    tendencies = tendency(padded)
    block_row = device * band_rows // BLK
    row_blocks = block_row * columns + jnp.arange(columns, dtype=jnp.int32)
    owner_map = jnp.sum(
        (ice_table[:, :, None] == row_blocks[None, None, :]).astype(jnp.float32), axis=1
    )
    surface = ocean_state[:, 0]
    strips = surface.reshape(3, band_rows, columns, BLK)
    packets = jnp.einsum("ob,frbc->forc", owner_map, strips, precision=lax.Precision.HIGHEST)
    arrived = lax.all_to_all(packets, "tiles", split_axis=1, concat_axis=1, tiled=True)
    my_blocks = lax.dynamic_index_in_dim(ice_table, device, 0, keepdims=False)
    present = my_blocks >= 0
    block_rows = jnp.where(present, my_blocks, 0) // columns
    gathered = []
    for slot_index in range(slot_count):
        rows_piece = lax.dynamic_slice_in_dim(arrived, block_rows[slot_index] * sources, sources, 1)
        gathered.append(rows_piece.reshape(rows_piece.shape[0], BLK, BLK))
    local_fields = jnp.stack(gathered)
    dynamics_next, stress_x, stress_y, ice_cover = jax.vmap(ice_block)(
        local_fields[:, -2:], ice_thickness, ice_dynamics
    )
    first_field = HEAT_RATE * ice_cover * (FREEZING - local_fields[:, 0])
    returned = jnp.stack([first_field, stress_x, stress_y], axis=1)
    ice_next = jnp.where(present[:, None, None, None], dynamics_next, 0.0)
    replies = jnp.zeros((3, owners, band_rows, BLK), jnp.float32)
    for slot_index in range(slot_count):
        first_source = block_rows[slot_index] * sources
        region = lax.dynamic_slice_in_dim(replies, first_source, sources, 1)
        update = jnp.where(
            present[slot_index], returned[slot_index].reshape(3, sources, band_rows, BLK), region
        )
        replies = lax.dynamic_update_slice_in_dim(replies, update, first_source, 1)
    answers = lax.all_to_all(replies, "tiles", split_axis=1, concat_axis=1, tiled=True)
    forcing = jnp.einsum(
        "ob,forc->frbc", owner_map, answers, precision=lax.Precision.HIGHEST
    ).reshape(3, band_rows, band_width)
    forcing_gain = jnp.asarray((1.0, STRESS_GAIN, STRESS_GAIN), dtype=surface.dtype).reshape(
        3, 1, 1
    )
    forcing = forcing * forcing_gain
    tendencies = tendencies.at[:, 0].add(forcing)
    land_row = lax.dynamic_slice_in_dim(land_mask, block_row * columns, columns, 0)
    wet_blocks = 1.0 - land_row.astype(jnp.float32)
    wet_cells = jnp.broadcast_to(wet_blocks[None, :, None], (band_rows, columns, BLK)).reshape(
        band_rows, band_width
    )
    keep_mask = jnp.stack([jnp.ones_like(wet_cells), wet_cells, wet_cells])[:, None]
    ocean_next = (ocean_state + TIME_STEP * wet_cells * tendencies) * keep_mask
    return (ocean_next, ice_next)


def solution(mesh):
    in_specs = (
        P(None, "groups", "tiles", None),
        P("tiles", "groups", None, None),
        P("tiles", "groups", None, None),
        P("groups", None),
        P("groups"),
    )
    out_specs = (P(None, "groups", "tiles", None), P("tiles", "groups", None, None))
    return jax.shard_map(shards, mesh=mesh, in_specs=in_specs, out_specs=out_specs, check_vma=False)
```

profile of v0, /device:TPU:0, one launch (start us, length us, event | category | flops | bytes accessed | tf_op | source)
XLA Modules:
  0.0 78.4 jit_solution(3959097477088898651)
XLA Ops:
  0.6 2.3 %fusion.280 = (f32[3,2,1,4352]{3,2,0,1:T(1,128)}, f32[3,2,1,4352]{3,2,0,1:T(1,128)}) fusion(f32[3,2,16,4352]{3,2,1,0:T(8,128)} %param.9), kind=kLoop, calls=%fused_computation.517 | loop fusion | bytes 417792 | tf_op jit(solution)/shard_map/slice | solution.py:31
  2.9 1.3 %collective-permute-start = (f32[3,2,1,4352]{3,2,0,1:T(1,128)}, f32[3,2,1,4352]{3,2,0,1:T(1,128)}, u32[]{:S(2)}, u32[]{:S(2)}) collective-permute-start(f32[3,2,1,4352]{3,2,0,1:T(1,128)} %get-tuple-element.60), channel_id=1, source_target_pairs={{1,0},{2,1},{3,2},{4,3},{5,4},{6,5},{7,6},{8,7},{9,8},{10,9},{11,1... | collective-permute-start | bytes 313352 | tf_op jit(solution)/shard_map/ppermute | solution.py:36
  4.2 3.7 %collective-permute-start.1 = (f32[3,2,1,4352]{3,2,0,1:T(1,128)}, f32[3,2,1,4352]{3,2,0,1:T(1,128)}, u32[]{:S(2)}, u32[]{:S(2)}) collective-permute-start(f32[3,2,1,4352]{3,2,0,1:T(1,128)} %get-tuple-element.59), channel_id=1, source_target_pairs={{0,1},{1,2},{2,3},{3,4},{4,5},{5,6},{6,7},{7,8},{8,9},{9,10},{10,1... | collective-permute-start | bytes 313352 | tf_op jit(solution)/shard_map/ppermute | solution.py:34
  7.9 2.5 %fusion.279 = (f32[3,1,16,4352]{3,2,0,1:T(8,128)S(1)}, f32[3,1,16,4352]{3,2,0,1:T(8,128)S(1)}, f32[3,1,16,4352]{3,2,0,1:T(8,128)}) fusion(f32[3,2,16,4352]{3,2,1,0:T(8,128)} %param.9), kind=kLoop, calls=%fused_computation.516 | loop fusion | flops 417792 | bytes 4177920 | tf_op jit(solution)/shard_map/slice | solution.py:128
  11.7 0.9 %copy.90 = f32[3,16,16,128]{3,2,0,1:T(8,128)} copy(f32[3,16,16,128]{3,1,2,0:T(8,128)S(1)} %convolution_bitcast_fusion.1) | data formatting | bytes 786432 | tf_op jit(solution)/shard_map/ob,frbc->forc/transpose | solution.py:151
  12.6 7.4 %all-to-all-start = ((f32[3,16,16,128]{3,2,0,1:T(8,128)}), f32[3,16,16,128]{3,2,0,1:T(8,128)}, u32[]{:S(2)}, u32[]{:S(2)}) async-start(f32[3,16,16,128]{3,2,0,1:T(8,128)} %copy.90), calls=%async_computation | async-start | bytes 786432 | tf_op jit(solution)/shard_map/all_to_all | solution.py:152
  20.0 1.2 %multiply_bitcast_fusion.1 = (f32[2,16,4352]{2,1,0:T(8,128)S(1)}, f32[1,2,16,4352]{3,2,0,1:T(8,128)}, f32[1,2,16,4352]{3,2,0,1:T(8,128)}, f32[2,16,4352]{2,1,0:T(8,128)}) fusion(f32[3,2,16,4352]{3,2,1,0:T(8,128)S(1)} %copy-done), kind=kLoop, calls=%fused_computation.17 | loop fusion | flops 417792 | bytes 3342336 | tf_op jit(solution)/shard_map/mul | solution.py:126
  21.3 1.3 %copy.102 = f32[3,2,16,4352]{3,2,0,1:T(8,128)} copy(f32[3,2,16,4352]{3,2,1,0:T(8,128)S(1)} %copy-done) | data formatting | bytes 3342336 | tf_op args[0]
  22.6 2.2 %fusion.281 = (f32[3,2,16,4351]{3,2,0,1:T(8,128)}, f32[3,2,16,4351]{3,2,0,1:T(8,128)}) fusion(f32[3,2,16,4352]{3,2,1,0:T(8,128)S(1)} %copy-done), kind=kLoop, calls=%fused_computation.518 | loop fusion | bytes 6683904 | tf_op jit(solution)/shard_map/jit(_roll_static)/slice | solution.py:121
  28.5 1.0 %slice_bitcast_fusion.1 = (f32[2,128,128]{2,1,0:T(8,128)S(1)}, f32[2,128,128]{2,1,0:T(8,128)S(1)}) fusion(f32[2,5,128,128]{3,2,1,0:T(8,128)} %param.10), kind=kLoop, calls=%fused_computation.498 | loop fusion | bytes 524288 | tf_op jit(solution)/shard_map/vmap()/squeeze | solution.py:63
  29.5 1.2 %fusion.267 = (f32[2,128,128]{2,1,0:T(8,128)S(1)}, f32[2,128,128]{2,1,0:T(8,128)S(1)}) fusion(f32[2,5,128,128]{3,2,1,0:T(8,128)} %param.11, f32[5]{0:T(128)S(1)} %copy-done.11), kind=kLoop, calls=%fused_computation.515 | loop fusion | flops 425984 | bytes 917524 | tf_op jit(solution)/shard_map/vmap()/reduce_sum | solution.py:59
  30.7 1.8 %fusion.261 = (f32[2,128,128]{2,1,0:T(8,128)}, f32[2,128,128]{2,1,0:T(8,128)S(1)}, f32[2,128,128]{2,1,0:T(8,128)S(1)}) fusion(f32[2,5,128,128]{3,2,1,0:T(8,128)} %param.10, f32[2,128,128]{2,1,0:T(8,128)S(1)} %get-tuple-element.80, f32[2,128,128]{2,1,0:T(8,128)S(1)} %get-tuple-element.79, f32[2,128,128]{2,1,0:T(8,128)S(1)} %get-tuple-element.21), kind=kLoop, calls=%fused_computation.448 | loop fusion | flops 983040 | bytes 917504 | tf_op jit(solution)/shard_map/vmap()/add | solution.py:86
  32.6 1.8 %fusion.259 = (f32[2,128,128]{2,1,0:T(8,128)}, f32[2,128,128]{2,1,0:T(8,128)}) fusion(f32[2,128,128]{2,1,0:T(8,128)S(1)} %get-tuple-element.51, f32[2,5,128,128]{3,2,1,0:T(8,128)} %param.10, f32[2,128,128]{2,1,0:T(8,128)S(1)} %get-tuple-element.50, f32[2,128,128]{2,1,0:T(8,128)S(1)} %get-tuple-element.21, f32[2,128,128]{2,1,0:T(8,128)S(1)} %get-tuple-element.80, ...), kind=kLoop, calls=%fused_computation.445 | loop fusion | flops 524288 | bytes 1179648 | tf_op jit(solution)/shard_map/vmap()/add | solution.py:87
  34.3 1.0 %pad_maximum_fusion.4 = f32[3,16,4352]{2,1,0:T(8,128)} fusion(f32[1,16,4352]{2,1,0:T(8,128)S(1)} %broadcast_in_dim.36, f32[3]{0:T(128)S(1)} %pad.326.clone), kind=kLoop, calls=%fused_computation.11 | loop fusion | flops 417792 | bytes 1114124 | tf_op jit(solution)/shard_map/stack | solution.py:189
  36.1 6.2 %fusion = f32[3,2,16,4352]{3,2,0,1:T(8,128)} fusion(f32[1,2,16,4352]{3,2,0,1:T(8,128)S(1)} %copy-done.4, f32[1,2,16,4352]{3,2,0,1:T(8,128)} %get-tuple-element.57, f32[3,1,16,4352]{3,2,0,1:T(8,128)S(1)} %get-tuple-element.53, f32[3,1,16,4352]{3,2,0,1:T(8,128)S(1)} %copy-done.3, f32[3,2,16,4352]{3,2,0,1:T(8,128)} %copy.102, ...), kind=kLoop, calls=%fused_computation.5 | loop fusion | flops 9609216 | bytes 10792972 | tf_op jit(solution)/shard_map/add | solution.py:131
  42.3 1.1 %constant_dynamic-slice_fusion.1 = (f32[3,8,16,128]{3,2,0,1:T(8,128)S(1)}, f32[3,8,16,128]{3,2,0,1:T(8,128)S(1)}) fusion(f32[3,16,16,128]{3,2,0,1:T(8,128)} %all-to-all-done, s32[]{:T(128)S(6)} %select_n.60, s32[]{:T(128)S(6)} %select_n.61), kind=kLoop, calls=%fused_computation.509 | loop fusion | bytes 786440 | tf_op jit(solution)/shard_map/dynamic_slice | solution.py:158
  51.2 0.8 copy.100
  51.9 6.0 %all-to-all-start.1 = ((f32[3,16,16,128]{3,2,0,1:T(8,128)}), f32[3,16,16,128]{3,2,0,1:T(8,128)}, u32[]{:S(2)}, u32[]{:S(2)}) async-start(f32[3,16,16,128]{3,2,0,1:T(8,128)} %copy.100), calls=%async_computation.1 | async-start | bytes 786432 | tf_op jit(solution)/shard_map/all_to_all | solution.py:175
  58.1 0.9 %copy.104 = f32[2,5,128,128]{3,2,1,0:T(8,128)} copy(f32[2,5,128,128]{3,2,0,1:T(8,128)S(1)} %select_bitcast_fusion) | data formatting | bytes 1310720
  59.0 11.2 %all-to-all-done.1 = f32[3,16,16,128]{3,2,0,1:T(8,128)} async-done(((f32[3,16,16,128]{3,2,0,1:T(8,128)}), f32[3,16,16,128]{3,2,0,1:T(8,128)}, u32[]{:S(2)}, u32[]{:S(2)}) %all-to-all-start.1) | async-done | bytes 393248 | tf_op jit(solution)/shard_map/all_to_all | solution.py:175
  70.2 2.9 %convolution_bitcast_fusion = f32[3,16,34,128]{3,2,1,0:T(8,128)} fusion(f32[3,16,16,128]{3,2,0,1:T(8,128)} %all-to-all-done.1, f32[16,34]{1,0:T(8,128)S(1)} %convert_reduce_fusion), kind=kOutput, calls=%fused_computation.7 | convolution fusion | flops 40108032 | bytes 1230976 | tf_op jit(solution)/shard_map/ob,forc->frbc/dot_general | solution.py:176
  73.1 2.2 %reshape.109 = f32[3,1,16,4352]{3,2,0,1:T(8,128)} reshape(f32[3,16,34,128]{3,2,1,0:T(8,128)} %convolution_bitcast_fusion) | data formatting | bytes 1671168 | tf_op jit(solution)/shard_map/reshape | solution.py:178
  75.4 1.4 %fusion.1 = f32[3,2,16,4352]{3,2,0,1:T(8,128)S(1)} fusion(f32[3,2,16,4352]{3,2,0,1:T(8,128)S(1)} %copy-done.1, f32[3,1,16,4352]{3,2,0,1:T(8,128)} %reshape.109, f32[3]{0:T(128)S(1)} %copy-done.12), kind=kLoop, calls=%fused_computation.10 | loop fusion | flops 417792 | bytes 2507264 | tf_op jit(solution)/shard_map/scatter-add | solution.py:183
  77.1 1.3 %copy.103 = f32[3,2,16,4352]{3,2,1,0:T(8,128)} copy(f32[3,2,16,4352]{3,2,0,1:T(8,128)S(1)} %add_multiply_fusion) | data formatting | bytes 3342336
  (85 shorter events, 12.4 us)
Async XLA Ops:
  2.9 33.2 %collective-permute-start = (f32[3,2,1,4352]{3,2,0,1:T(1,128)}, f32[3,2,1,4352]{3,2,0,1:T(1,128)}, u32[]{:S(2)}, u32[]{:S(2)}) collective-permute-start(f32[3,2,1,4352]{3,2,0,1:T(1,128)} %get-tuple-element.60), channel_id=1, source_target_pairs={{1,0},{2,1},{3,2},{4,3},{5,4},{6,5},{7,6},{8,7},{9,8},{10,9},{11,1... | collective-permute-start | bytes 313352 | tf_op jit(solution)/shard_map/ppermute | solution.py:36
  4.2 31.9 %collective-permute-start.1 = (f32[3,2,1,4352]{3,2,0,1:T(1,128)}, f32[3,2,1,4352]{3,2,0,1:T(1,128)}, u32[]{:S(2)}, u32[]{:S(2)}) collective-permute-start(f32[3,2,1,4352]{3,2,0,1:T(1,128)} %get-tuple-element.59), channel_id=1, source_target_pairs={{0,1},{1,2},{2,3},{3,4},{4,5},{5,6},{6,7},{7,8},{8,9},{9,10},{10,1... | collective-permute-start | bytes 313352 | tf_op jit(solution)/shard_map/ppermute | solution.py:34
  10.3 0.7 copy-start.10
  10.5 9.6 %copy-start = (f32[3,2,16,4352]{3,2,1,0:T(8,128)S(1)}, f32[3,2,16,4352]{3,2,1,0:T(8,128)}, u32[]{:S(2)}) copy-start(f32[3,2,16,4352]{3,2,1,0:T(8,128)} %param.9) | copy-start | bytes 5013508
  12.6 29.7 %all-to-all-start = ((f32[3,16,16,128]{3,2,0,1:T(8,128)}), f32[3,16,16,128]{3,2,0,1:T(8,128)}, u32[]{:S(2)}, u32[]{:S(2)}) async-start(f32[3,16,16,128]{3,2,0,1:T(8,128)} %copy.90), calls=%async_computation | async-start | bytes 786432 | tf_op jit(solution)/shard_map/all_to_all | solution.py:152
  22.6 5.1 %copy-start.13 = (s32[68]{0:T(128)S(1)}, s32[68]{0:T(128)}, u32[]{:S(2)}) copy-start(s32[68]{0:T(128)} %param.13) | copy-start | bytes 820
  22.6 6.9 %copy-start.11 = (f32[5]{0:T(128)S(1)}, f32[5]{0:T(128)}, u32[]{:S(2)}) copy-start(f32[5]{0:T(128)} %constant.131.clone) | copy-start | bytes 64
  34.3 1.7 %copy-start.3 = (f32[3,1,16,4352]{3,2,0,1:T(8,128)S(1)}, f32[3,1,16,4352]{3,2,0,1:T(8,128)}, u32[]{:S(2)}) copy-start(f32[3,1,16,4352]{3,2,0,1:T(8,128)} %get-tuple-element.54) | copy-start | bytes 2506756
  34.3 1.7 %copy-start.4 = (f32[1,2,16,4352]{3,2,0,1:T(8,128)S(1)}, f32[1,2,16,4352]{3,2,0,1:T(8,128)}, u32[]{:S(2)}) copy-start(f32[1,2,16,4352]{3,2,0,1:T(8,128)} %get-tuple-element.56) | copy-start | bytes 1671172
  42.3 1.3 %copy-start.5 = (f32[2,5,128,128]{3,2,1,0:T(8,128)S(1)}, f32[2,5,128,128]{3,2,1,0:T(8,128)}, u32[]{:S(2)}) copy-start(f32[2,5,128,128]{3,2,1,0:T(8,128)} %param.10) | copy-start | bytes 1966084
  42.3 1.3 %copy-start.6 = (f32[2,128,128]{2,1,0:T(8,128)S(1)}, f32[2,128,128]{2,1,0:T(8,128)}, u32[]{:S(2)}) copy-start(f32[2,128,128]{2,1,0:T(8,128)} %get-tuple-element.77) | copy-start | bytes 393220
  42.3 1.3 %copy-start.7 = (f32[2,128,128]{2,1,0:T(8,128)S(1)}, f32[2,128,128]{2,1,0:T(8,128)}, u32[]{:S(2)}) copy-start(f32[2,128,128]{2,1,0:T(8,128)} %get-tuple-element.78) | copy-start | bytes 393220
  42.3 1.3 %copy-start.8 = (f32[2,128,128]{2,1,0:T(8,128)S(1)}, f32[2,128,128]{2,1,0:T(8,128)}, u32[]{:S(2)}) copy-start(f32[2,128,128]{2,1,0:T(8,128)} %get-tuple-element.49) | copy-start | bytes 393220
  51.9 18.3 %all-to-all-start.1 = ((f32[3,16,16,128]{3,2,0,1:T(8,128)}), f32[3,16,16,128]{3,2,0,1:T(8,128)}, u32[]{:S(2)}, u32[]{:S(2)}) async-start(f32[3,16,16,128]{3,2,0,1:T(8,128)} %copy.100), calls=%async_computation.1 | async-start | bytes 786432 | tf_op jit(solution)/shard_map/all_to_all | solution.py:175
  59.0 16.3 %copy-start.1 = (f32[3,2,16,4352]{3,2,0,1:T(8,128)S(1)}, f32[3,2,16,4352]{3,2,0,1:T(8,128)}, u32[]{:S(2)}) copy-start(f32[3,2,16,4352]{3,2,0,1:T(8,128)} %fusion) | copy-start | bytes 5013508
  59.0 16.3 %copy-start.12 = (f32[3]{0:T(128)S(1)}, f32[3]{0:T(128)}, u32[]{:S(2)}) copy-start(f32[3]{0:T(128)} %constant.132.clone) | copy-start | bytes 40
  75.4 1.5 %copy-start.2 = (f32[3,16,4352]{2,1,0:T(8,128)S(1)}, f32[3,16,4352]{2,1,0:T(8,128)}, u32[]{:S(2)}) copy-start(f32[3,16,4352]{2,1,0:T(8,128)} %pad_maximum_fusion.4) | copy-start | bytes 2506756
  75.4 1.5 %copy-start.9 = (f32[4352]{0:T(1024)S(1)}, f32[4352]{0:T(1024)}, u32[]{:S(2)}) copy-start(f32[4352]{0:T(1024)} %bitcast_multiply_fusion.3) | copy-start | bytes 52228
where the time goes:
time: 79.1 us; the launch traced here: 78.4 us
  other arithmetic  25.9 us (33%)
  starting transfers between devices  18.4 us (23%)
  local copies, waits for them, and re-layouts  17.1 us (22%)
  waiting for transfers between devices  11.2 us (14%)
  matrix products  3.51 us (4%)
  between operations  2.36 us (3%)
    all_to_all x1, waiting for transfers between devices, shards(): lax.all_to_all(replies, 'tiles', split_axis=1, concat_axis=1, tiled=True)  11.2 us
    all_to_all x1, starting transfers between devices, shards(): lax.all_to_all(packets, 'tiles', split_axis=1, concat_axis=1, tiled=True)  7.4 us
    add x1, other arithmetic, tendency(): MIX_HORIZ * laplace - advection + MIX_VERT * (upward_diff + downward_diff)  6.18 us
    all_to_all x1, starting transfers between devices, shards(): lax.all_to_all(replies, 'tiles', split_axis=1, concat_axis=1, tiled=True)  6.01 us
    unnamed x35, local copies, waits for them, and re-layouts  4.15 us
    ppermute x1, starting transfers between devices, padded_2(): lax.ppermute(tail, axis, [(i, (i + 1) % count) for i in range(ends)])  3.68 us
    add x7, other arithmetic, ice_block(): (1.0 - RELAXATION) * stress_diff + RELAXATION * (shear_viscosity * tension)  3.51 us
    slice x2, local copies, waits for them, and re-layouts, tendency(): east_cells = jnp.roll(centre, -1, axis=3)  2.91 us
  transfers between devices with their start and end apart: 4, of which 1 were waited for; matrix products, arithmetic and copies ran while one was open for 33% of the time, Pallas kernels for 0%

commit v1 on v0

v1 whole, which is shorter than its diff:
```python
import functools

import jax
import jax.numpy as jnp
from jax import lax
from jax.experimental import pallas as pl
from jax.experimental.pallas import tpu as pltpu
from jax.sharding import PartitionSpec as P

BLK = 128
NSUB = 8
TIME_STEP = 0.1
MIX_HORIZ = 0.5
MIX_VERT = 0.25
CORIOLIS = 0.5
STRESS_GAIN = 2.0
RELAXATION = 0.2
ICE_STEP = 0.5
STRENGTH_SCALE = 0.25
HEAT_RATE = 0.5
FREEZING = -1.0
CATEGORY_WEIGHTS = (0.5, 0.75, 1.0, 1.25, 1.5)
PAD = 8
STRIP = 32
MESH = pl.DeviceIdType.MESH


def loop(count, body):
    def step(i, carry):
        body(i)
        return carry

    lax.fori_loop(0, count, step, 0)


def kernel(
    n, columns, levels, slots, rows,
    table, land, ocean_h, dyn_h, thick_h, ocean_o, ice_o,
    oc, acc, dy, th, hs, hr, pk, ar, cpk, car, bpk, bar, st, cf, io, owner_of,
    load_sem, store_sem, ocean_sem, early_sem, late_sem, fs, fr, cs, cr, bs, br, hss, hrs,
):
    me = lax.axis_index("tiles")
    sources = BLK // rows
    block_rows = n // sources
    my_row = me // sources
    my_part = lax.rem(me, sources)
    base = my_row * columns

    def lanes(c):
        return pl.ds(pl.multiple_of(c * BLK, BLK), BLK)

    def load_ocean(c):
        return pltpu.make_async_copy(ocean_h.at[:, :, :, lanes(c)], oc.at[c], ocean_sem.at[c])

    load_thick = pltpu.make_async_copy(thick_h, th, load_sem.at[0])
    load_dyn = pltpu.make_async_copy(dyn_h, dy, load_sem.at[1])
    loop(columns, lambda c: load_ocean(c).start())
    load_thick.start()
    load_dyn.start()

    barrier = pltpu.get_barrier_semaphore()

    def greet(k):
        peer = lax.rem(me + 1 + k, n)
        pl.semaphore_signal(barrier, inc=1, device_id={"tiles": peer}, device_id_type=MESH)

    loop(n - 1, greet)

    def remote(src, dst, ssem, rsem, slot_there, peer):
        return pltpu.make_async_remote_copy(
            src_ref=src.at[peer], dst_ref=dst.at[slot_there], send_sem=ssem.at[peer],
            recv_sem=rsem.at[slot_there], device_id={"tiles": peer}, device_id_type=MESH,
        )

    def send(src, dst, ssem, rsem, peer):
        @pl.when(peer != me)
        def _():
            remote(src, dst, ssem, rsem, me, peer).start()

    def wait_recv(src, dst, ssem, rsem, peer):
        @pl.when(peer != me)
        def _():
            remote(src, dst, ssem, rsem, peer, peer).wait_recv()

    def wait_send(src, dst, ssem, rsem, peer):
        @pl.when(peer != me)
        def _():
            remote(src, dst, ssem, rsem, me, peer).wait_send()

    def member(row, i):
        return row * sources + lax.rem(my_part + i, sources)

    def row_of(j):
        return lax.rem(my_row + j, block_rows)

    loop(columns, lambda c: load_ocean(c).wait())

    def pack(o):
        col = 0
        for s in range(slots):
            rel = table[o, s] - base
            col = jnp.where((rel >= 0) & (rel < columns), rel, col)
        pk[o, 0] = oc[col, 1, 0]
        pk[o, 1] = oc[col, 2, 0]

    loop(n, pack)
    ar[me] = pk[me]
    blank = jnp.zeros((1, BLK), jnp.float32)

    def edges(c):
        tops = [oc[c, f, k, rows - 1 : rows] for f in range(3) for k in range(levels)]
        ends = [oc[c, f, k, 0:1] for f in range(3) for k in range(levels)]
        more = [blank] * (hs.shape[2] - len(tops))
        hs[0, c] = jnp.concatenate(tops + more, axis=0)
        hs[1, c] = jnp.concatenate(ends + more, axis=0)

    loop(columns, edges)

    pl.semaphore_wait(barrier, n - 1)

    def send_fwd(q):
        send(pk, ar, fs, fr, member(row_of(1 + q // sources), lax.rem(q, sources)))

    loop(n, send_fwd)

    def halo(i, peer):
        return pltpu.make_async_remote_copy(
            src_ref=hs.at[i], dst_ref=hr.at[i], send_sem=hss.at[i], recv_sem=hrs.at[i],
            device_id={"tiles": peer}, device_id_type=MESH,
        )

    up = jnp.minimum(me + 1, n - 1)
    down = jnp.maximum(me - 1, 0)

    @pl.when(me < n - 1)
    def _():
        halo(0, up).start()

    @pl.when(me > 0)
    def _():
        halo(1, down).start()

    @pl.when(me == 0)
    def _():
        hr[0] = jnp.zeros(hr.shape[1:], jnp.float32)

    @pl.when(me == n - 1)
    def _():
        hr[1] = jnp.zeros(hr.shape[1:], jnp.float32)

    def find(row):
        slot = jnp.int32(0)
        valid = jnp.int32(0)
        for s in range(slots):
            rel = table[me, s] - row * columns
            hit = (rel >= 0) & (rel < columns)
            slot = jnp.where(hit, s, slot)
            valid = jnp.where(hit, 1, valid)
        return slot, valid

    load_thick.wait()
    load_dyn.wait()

    def prepare(j):
        row = row_of(j)
        slot, valid = find(row)
        keep = valid.astype(jnp.float32)
        for r in range(0, BLK, STRIP):
            cut = pl.ds(r, STRIP)
            parts = [th[slot, k, cut, :] for k in range(len(CATEGORY_WEIGHTS))]
            total = parts[0]
            weighted = CATEGORY_WEIGHTS[0] * parts[0]
            for weight, part in zip(CATEGORY_WEIGHTS[1:], parts[1:]):
                total = total + part
                weighted = weighted + weight * part
            cf[j, 0, cut, :] = total
            cf[j, 1, cut, :] = (0.5 * RELAXATION * STRENGTH_SCALE) * weighted
            cover = keep * (1.0 - jnp.exp(-total))
            for i in range(STRIP // rows):
                cpk[row * sources + r // rows + i] = cover[i * rows : (i + 1) * rows]
            for f in range(5):
                st[j, f, pl.ds(PAD + r, STRIP), :] = dy[slot, f, cut, :]
        for f in range(5):
            st[j, f, 0:PAD, :] = jnp.zeros((PAD, BLK), jnp.float32)
            st[j, f, PAD + BLK :, :] = jnp.zeros((PAD, BLK), jnp.float32)

    def prepare_and_send(q):
        j = lax.rem(q + 1, block_rows)
        prepare(j)
        loop(sources, lambda i: send(cpk, car, cs, cr, member(row_of(j), i)))

    loop(block_rows, prepare_and_send)
    car[me] = cpk[me]
    car[n] = jnp.zeros(car.shape[1:], jnp.float32)
    bar[n] = jnp.zeros(bar.shape[1:], jnp.float32)

    def inverse(c):
        def look(o, found):
            for s in range(slots):
                found = jnp.where(table[o, s] == base + c, o, found)
            return found

        found = jnp.int32(n)
        if n <= 32:
            for o in range(n):
                found = look(o, found)
        else:
            found = lax.fori_loop(0, n, look, found)
        owner_of[c] = found

    loop(columns, inverse)

    lane = lax.broadcasted_iota(jnp.int32, (STRIP, BLK), 1)
    not_last = lane < BLK - 1
    not_first = lane > 0

    def east(x):
        return jnp.where(not_last, pltpu.roll(x, BLK - 1, 1), 0.0) - jnp.where(
            not_first, pltpu.roll(x, 1, 1), 0.0
        )

    def ice(j):
        row = row_of(j)
        first = row * sources

        def get(f, r, shift=0):
            return st[j, f, pl.ds(PAD + r + shift, STRIP), :]

        def north(f, r):
            return get(f, r, 1) - get(f, r, -1)

        def water(f, r):
            return ar[pl.ds(first + r // rows, STRIP // rows), f].reshape(STRIP, BLK)

        def substep(step):
            for r in range(0, BLK, STRIP):
                cut = pl.ds(r, STRIP)
                eu = east(get(0, r))
                ev = east(get(1, r))
                nu = north(0, r)
                nv = north(1, r)
                div = eu + nv
                ten = eu - nv
                shear = nu + ev
                scale = cf[j, 1, cut, :]
                z = scale * lax.rsqrt(div * div + 0.25 * (ten * ten + shear * shear) + 1.0)
                z4 = 0.25 * z
                mine = pl.ds(PAD + r, STRIP)
                st[j, 2, mine, :] = (1.0 - RELAXATION) * get(2, r) + (z * div - scale)
                st[j, 3, mine, :] = (1.0 - RELAXATION) * get(3, r) + z4 * ten
                st[j, 4, mine, :] = (1.0 - RELAXATION) * get(4, r) + z4 * shear
            for r in range(0, BLK, STRIP):
                cut = pl.ds(r, STRIP)
                fx = 0.25 * east(get(2, r) + get(3, r)) + 0.5 * north(4, r)
                fy = 0.25 * (north(2, r) - north(3, r)) + 0.5 * east(get(4, r))
                u = get(0, r)
                v = get(1, r)
                uo = water(0, r)
                vo = water(1, r)
                total = cf[j, 0, cut, :]
                ru = uo - u
                rv = vo - v
                q = ru * ru + rv * rv + 0.0001
                drag = q * lax.rsqrt(q)
                inertia = total * (1.0 / ICE_STEP)
                turn = CORIOLIS * total
                inv = 1.0 / (inertia + drag)
                mine = pl.ds(PAD + r, STRIP)
                st[j, 0, mine, :] = (inertia * u + fx + drag * uo + turn * v) * inv
                st[j, 1, mine, :] = (inertia * v + fy + drag * vo - turn * u) * inv

        loop(NSUB, substep)
        slot, valid = find(row)
        keep = valid.astype(jnp.float32)
        for r in range(0, BLK, STRIP):
            u = get(0, r)
            v = get(1, r)
            ru = u - water(0, r)
            rv = v - water(1, r)
            q = ru * ru + rv * rv + 0.0001
            drag = keep * (q * lax.rsqrt(q))
            taux = drag * ru
            tauy = drag * rv
            for i in range(STRIP // rows):
                bpk[first + r // rows + i, 0] = taux[i * rows : (i + 1) * rows]
                bpk[first + r // rows + i, 1] = tauy[i * rows : (i + 1) * rows]

    def item(j):
        loop(sources, lambda i: wait_recv(pk, ar, fs, fr, member(row_of(j), i)))
        ice(j)
        loop(sources, lambda i: send(bpk, bar, bs, br, member(row_of(j), i)))

    loop(block_rows, item)
    bar[me] = bpk[me]

    def finish_ice(s):
        block = table[me, s]
        j = jnp.int32(0)
        for other in range(block_rows):
            rel = block - row_of(other) * columns
            j = jnp.where((rel >= 0) & (rel < columns), other, j)
        keep = jnp.where(block >= 0, 1, 0).astype(jnp.float32)
        for f in range(5):
            io[s, f] = keep * st[j, f, pl.ds(PAD, BLK), :]

    loop(slots, finish_ice)
    store_ice = pltpu.make_async_copy(io, ice_o, store_sem.at[0])
    store_ice.start()

    @pl.when(me < n - 1)
    def _():
        halo(0, up).wait_send()
        halo(1, up).wait_recv()

    @pl.when(me > 0)
    def _():
        halo(1, down).wait_send()
        halo(0, down).wait_recv()

    lane_o = lax.broadcasted_iota(jnp.int32, (rows, BLK), 1)
    row_o = lax.broadcasted_iota(jnp.int32, (rows, BLK), 0)

    def tend(c):
        left = lax.rem(c + columns - 1, columns)
        right = lax.rem(c + 1, columns)
        wet = 1.0 - land[base + c].astype(jnp.float32)
        gain = TIME_STEP * wet
        x = [[oc[c, f, k] for k in range(levels)] for f in range(3)]
        for k in range(levels):
            for f in range(3):
                at = f * levels + k
                centre = x[f][k]
                east_cells = jnp.where(
                    lane_o == BLK - 1,
                    pltpu.roll(oc[right, f, k], BLK - 1, 1),
                    pltpu.roll(centre, BLK - 1, 1),
                )
                west_cells = jnp.where(
                    lane_o == 0, pltpu.roll(oc[left, f, k], 1, 1), pltpu.roll(centre, 1, 1)
                )
                upper = jnp.where(
                    row_o == rows - 1, hr[1, c, at : at + 1], pltpu.roll(centre, rows - 1, 0)
                )
                lower = jnp.where(row_o == 0, hr[0, c, at : at + 1], pltpu.roll(centre, 1, 0))
                laplace = upper + lower + east_cells + west_cells - 4.0 * centre
                advection = x[1][k] * (0.5 * (east_cells - west_cells)) + x[2][k] * (
                    0.5 * (upper - lower)
                )
                t = MIX_HORIZ * laplace - advection
                if k + 1 < levels:
                    t = t + MIX_VERT * (x[f][k + 1] - centre)
                if k > 0:
                    t = t + MIX_VERT * (x[f][k - 1] - centre)
                if f == 1:
                    t = t + CORIOLIS * x[2][k]
                if f == 2:
                    t = t - CORIOLIS * x[1][k]
                result = centre + gain * t
                acc[c, f, k] = result * wet if f else result

    loop(columns, tend)

    loop(n, lambda d: wait_recv(cpk, car, cs, cr, d))

    def store_early(c):
        return pltpu.make_async_copy(acc.at[c, 0], ocean_o.at[0, :, :, lanes(c)], early_sem.at[c])

    def store_late(c):
        return pltpu.make_async_copy(
            acc.at[c, 1:3], ocean_o.at[1:3, :, :, lanes(c)], late_sem.at[c]
        )

    def heat(c):
        wet = 1.0 - land[base + c].astype(jnp.float32)
        cover = car[owner_of[c]]
        acc[c, 0, 0] += (TIME_STEP * HEAT_RATE * wet) * (cover * (FREEZING - oc[c, 0, 0]))
        store_early(c).start()

    loop(columns, heat)
    loop(n, lambda d: wait_recv(bpk, bar, bs, br, d))

    def stress(c):
        wet = 1.0 - land[base + c].astype(jnp.float32)
        o = owner_of[c]
        for f in range(2):
            acc[c, 1 + f, 0] += (TIME_STEP * STRESS_GAIN * wet) * bar[o, f]
        store_late(c).start()

    loop(columns, stress)

    def drain(d):
        wait_send(pk, ar, fs, fr, d)
        wait_send(cpk, car, cs, cr, d)
        wait_send(bpk, bar, bs, br, d)

    loop(n, drain)
    store_ice.wait()
    loop(columns, lambda c: store_early(c).wait())
    loop(columns, lambda c: store_late(c).wait())


def shards(n, ocean_state, ice_dynamics, ice_thickness, ice_table, land_mask):
    _, levels, rows, width = ocean_state.shape
    slots = ice_dynamics.shape[0]
    columns = width // BLK
    block_rows = n * rows // BLK
    f32 = jnp.float32
    halo_rows = -(-3 * levels // 8) * 8
    dma = pltpu.SemaphoreType.DMA
    smem = pl.BlockSpec(memory_space=pltpu.SMEM)
    hbm = pl.BlockSpec(memory_space=pl.ANY)
    return pl.pallas_call(
        functools.partial(kernel, n, columns, levels, slots, rows),
        out_shape=(
            jax.ShapeDtypeStruct(ocean_state.shape, f32),
            jax.ShapeDtypeStruct(ice_dynamics.shape, f32),
        ),
        in_specs=[smem, smem, hbm, hbm, hbm],
        out_specs=(hbm, hbm),
        scratch_shapes=[
            pltpu.VMEM((columns, 3, levels, rows, BLK), f32),
            pltpu.VMEM((columns, 3, levels, rows, BLK), f32),
            pltpu.VMEM(ice_dynamics.shape, f32),
            pltpu.VMEM(ice_thickness.shape, f32),
            pltpu.VMEM((2, columns, halo_rows, BLK), f32),
            pltpu.VMEM((2, columns, halo_rows, BLK), f32),
            pltpu.VMEM((n, 2, rows, BLK), f32),
            pltpu.VMEM((n, 2, rows, BLK), f32),
            pltpu.VMEM((n, rows, BLK), f32),
            pltpu.VMEM((n + 1, rows, BLK), f32),
            pltpu.VMEM((n, 2, rows, BLK), f32),
            pltpu.VMEM((n + 1, 2, rows, BLK), f32),
            pltpu.VMEM((block_rows, 5, BLK + 2 * PAD, BLK), f32),
            pltpu.VMEM((block_rows, 2, BLK, BLK), f32),
            pltpu.VMEM(ice_dynamics.shape, f32),
            pltpu.SMEM((columns,), jnp.int32),
            dma((2,)), dma((1,)), dma((columns,)), dma((columns,)), dma((columns,)),
            dma((n,)), dma((n,)), dma((n,)), dma((n,)), dma((n,)), dma((n,)),
            dma((2,)), dma((2,)),
        ],
        compiler_params=pltpu.CompilerParams(
            collective_id=0, has_side_effects=True, vmem_limit_bytes=48 * 1024 * 1024
        ),
    )(ice_table, land_mask, ocean_state, ice_dynamics, ice_thickness)


def solution(mesh):
    in_specs = (
        P(None, "groups", "tiles", None),
        P("tiles", "groups", None, None),
        P("tiles", "groups", None, None),
        P("groups", None),
        P("groups"),
    )
    out_specs = (P(None, "groups", "tiles", None), P("tiles", "groups", None, None))
    return jax.shard_map(
        functools.partial(shards, mesh.shape["tiles"]),
        mesh=mesh, in_specs=in_specs, out_specs=out_specs, check_vma=False,
    )
```

time: 79.1 us -> 36.6 us (0.46)
  Pallas kernels: 0 us -> 28.6 us
  other arithmetic: 25.9 us -> 0 us
  starting transfers between devices: 18.4 us -> 0 us
  waiting for transfers between devices: 11.2 us -> 0 us
  local copies, waits for them, and re-layouts: 17.1 us -> 7.04 us
  matrix products: 3.51 us -> 0 us
  between operations: 2.36 us -> 0.64 us
    pallas_call x0 -> x1, Pallas kernels: none -> 28.6 us  [shards(): pl.pallas_call(functools.partial(kernel, n, columns, levels, slots, rows)...]
    all_to_all x2 -> x0, starting transfers between devices: 13.4 us -> none  [the longest x1 7.4 us: shards(): lax.all_to_all(packets, 'tiles', split_axis=1, concat_axis=1, tiled=True)]
    add x18 -> x0, other arithmetic: 12.8 us -> none  [the longest x1 6.18 us: tendency(): MIX_HORIZ * laplace - advection + MIX_VERT * (upward_diff + downward_diff)]
    all_to_all x2 -> x0, waiting for transfers between devices: 11.2 us -> none  [the longest x1 11.2 us: shards(): lax.all_to_all(replies, 'tiles', split_axis=1, concat_axis=1, tiled=True)]
    slice x5 -> x0, local copies, waits for them, and re-layouts: 6.44 us -> none  [the longest x2 2.91 us: tendency(): east_cells = jnp.roll(centre, -1, axis=3)]
    ppermute x2 -> x0, starting transfers between devices: 4.96 us -> none  [the longest x1 3.68 us: padded_2(): lax.ppermute(tail, axis, [(i, (i + 1) % count) for i in range(ends)])]
    dot_general x2 -> x0, matrix products: 3.51 us -> none  [the longest x1 2.91 us: shards(): jnp.einsum('ob,forc->frbc', owner_map, answers, precision=lax.Precision.H...]
    slice x2 -> x0, other arithmetic: 3.07 us -> none  [the longest x1 2.47 us: tendency(): centre[:, :-1]]
  transfers between devices with their start and end apart: 4 -> 0, of which waited for: 1 -> 0; matrix products, arithmetic and copies ran while one was open for 33% -> 0% of each run, Pallas kernels for 0% -> 0%
where the time goes in v1:
time: 36.6 us; the launch traced here: 36.3 us
  Pallas kernels  28.6 us (78%)
  local copies, waits for them, and re-layouts  7.04 us (19%)
  between operations  0.64 us (2%)
    pallas_call x1, Pallas kernels, shards(): pl.pallas_call(functools.partial(kernel, n, columns, levels, slots, rows)...  28.6 us
    unnamed x11, local copies, waits for them, and re-layouts  7.04 us

profile of v1, /device:TPU:0, one launch (start us, length us, event | category | flops | bytes accessed | tf_op | source)
XLA Modules:
  0.0 36.3 jit_solution(6663511755227165657)
XLA Ops:
  0.6 0.8 %copy.7.table = s32[16,2]{1,0:T(8,128)S(1)} copy(s32[16,2]{0,1:T(2,128)} %param.8) | data formatting | bytes 256 | tf_op args[3]
  1.4 0.0 copy-start
  1.4 1.4 %copy-done = f32[3,2,16,4352]{3,2,1,0:T(8,128)S(1)} copy-done((f32[3,2,16,4352]{3,2,1,0:T(8,128)S(1)}, f32[3,2,16,4352]{3,2,1,0:T(8,128)}, u32[]{:S(2)}) %copy-start) | copy-done | bytes 1671192
  2.8 0.0 copy-start.1
  2.8 1.1 %copy-done.1 = f32[2,5,128,128]{3,2,1,0:T(8,128)S(1)} copy-done((f32[2,5,128,128]{3,2,1,0:T(8,128)S(1)}, f32[2,5,128,128]{3,2,1,0:T(8,128)}, u32[]{:S(2)}) %copy-start.1) | copy-done | bytes 655384
  3.9 0.0 copy-start.2
  3.9 1.1 %copy-done.2 = f32[2,5,128,128]{3,2,1,0:T(8,128)S(1)} copy-done((f32[2,5,128,128]{3,2,1,0:T(8,128)S(1)}, f32[2,5,128,128]{3,2,1,0:T(8,128)}, u32[]{:S(2)}) %copy-start.2) | copy-done | bytes 655384
  5.0 0.0 copy-start.3
  5.0 0.7 %copy-done.3 = s32[68]{0:T(128)S(1)} copy-done((s32[68]{0:T(128)S(1)}, s32[68]{0:T(128)}, u32[]{:S(2)}) %copy-start.3) | copy-done | bytes 296
  5.7 28.6 %shard_map.68 = (f32[3,2,16,4352]{3,2,1,0:T(8,128)S(1)}, f32[2,5,128,128]{3,2,1,0:T(8,128)S(1)}) custom-call(s32[16,2]{1,0:T(8,128)S(1)} %copy.7.table, s32[68]{0:T(128)S(1)} %copy-done.3, f32[3,2,16,4352]{3,2,1,0:T(8,128)S(1)} %copy-done, f32[2,5,128,128]{3,2,1,0:T(8,128)S(1)} %copy-done.1, f32[2,5,128,128]{3,2,1,0:T(8,128)S(1)} %copy-done.2), custom_call_target="tpu_custom_call" | custom-call | tf_op jit(solution)/shard_map/pallas_call | solution.py:412
  34.3 1.2 %copy.10 = f32[3,2,16,4352]{3,2,1,0:T(8,128)} copy(f32[3,2,16,4352]{3,2,1,0:T(8,128)S(1)} %get-tuple-element.4) | data formatting | bytes 3342336
  35.5 0.8 %copy.11 = f32[2,5,128,128]{3,2,1,0:T(8,128)} copy(f32[2,5,128,128]{3,2,1,0:T(8,128)S(1)} %get-tuple-element.5) | data formatting | bytes 1310720
Async XLA Ops:
  1.4 1.4 %copy-start = (f32[3,2,16,4352]{3,2,1,0:T(8,128)S(1)}, f32[3,2,16,4352]{3,2,1,0:T(8,128)}, u32[]{:S(2)}) copy-start(f32[3,2,16,4352]{3,2,1,0:T(8,128)} %ocean_h.1) | copy-start | bytes 5013508
  2.8 1.1 %copy-start.1 = (f32[2,5,128,128]{3,2,1,0:T(8,128)S(1)}, f32[2,5,128,128]{3,2,1,0:T(8,128)}, u32[]{:S(2)}) copy-start(f32[2,5,128,128]{3,2,1,0:T(8,128)} %dyn_h.1) | copy-start | bytes 1966084
  3.9 1.1 %copy-start.2 = (f32[2,5,128,128]{3,2,1,0:T(8,128)S(1)}, f32[2,5,128,128]{3,2,1,0:T(8,128)}, u32[]{:S(2)}) copy-start(f32[2,5,128,128]{3,2,1,0:T(8,128)} %thick_h.1) | copy-start | bytes 1966084
  5.0 0.7 %copy-start.3 = (s32[68]{0:T(128)S(1)}, s32[68]{0:T(128)}, u32[]{:S(2)}) copy-start(s32[68]{0:T(128)} %land.1) | copy-start | bytes 820

commit v2 on v1

--- a/solution.py
+++ b/solution.py
@@ -22,6 +22,7 @@
 CATEGORY_WEIGHTS = (0.5, 0.75, 1.0, 1.25, 1.5)
 PAD = 8
 STRIP = 32
+VMEM_BYTES = 64 * 1024 * 1024
 MESH = pl.DeviceIdType.MESH
 
 
@@ -35,9 +36,9 @@
 
 def kernel(
     n, columns, levels, slots, rows,
-    table, land, ocean_h, dyn_h, thick_h, ocean_o, ice_o,
-    oc, acc, dy, th, hs, hr, pk, ar, cpk, car, bpk, bar, st, cf, io, owner_of,
-    load_sem, store_sem, ocean_sem, early_sem, late_sem, fs, fr, cs, cr, bs, br, hss, hrs,
+    table_h, land_h, ocean_h, dyn_h, thick_h, acc, io,
+    oc, dy, th, hs, hr, pk, ar, cpk, car, bpk, bar, st, cf, owner_of, table, land,
+    load_sem, fs, fr, cs, cr, bs, br, hss, hrs,
 ):
     me = lax.axis_index("tiles")
     sources = BLK // rows
@@ -50,8 +51,12 @@
         return pl.ds(pl.multiple_of(c * BLK, BLK), BLK)
 
     def load_ocean(c):
-        return pltpu.make_async_copy(ocean_h.at[:, :, :, lanes(c)], oc.at[c], ocean_sem.at[c])
-
+        return pltpu.make_async_copy(ocean_h.at[:, :, :, lanes(c)], oc.at[c], load_sem.at[2])
+
+    load_table = pltpu.make_async_copy(table_h, table, load_sem.at[3])
+    load_land = pltpu.make_async_copy(land_h, land, load_sem.at[4])
+    load_table.start()
+    load_land.start()
     load_thick = pltpu.make_async_copy(thick_h, th, load_sem.at[0])
     load_dyn = pltpu.make_async_copy(dyn_h, dy, load_sem.at[1])
     loop(columns, lambda c: load_ocean(c).start())
@@ -93,12 +98,14 @@
     def row_of(j):
         return lax.rem(my_row + j, block_rows)
 
-    loop(columns, lambda c: load_ocean(c).wait())
+    load_table.wait()
+    load_land.wait()
+    pltpu.make_async_copy(oc, oc, load_sem.at[2]).wait()
 
     def pack(o):
         col = 0
         for s in range(slots):
-            rel = table[o, s] - base
+            rel = table[s, o] - base
             col = jnp.where((rel >= 0) & (rel < columns), rel, col)
         pk[o, 0] = oc[col, 1, 0]
         pk[o, 1] = oc[col, 2, 0]
@@ -152,7 +159,7 @@
         slot = jnp.int32(0)
         valid = jnp.int32(0)
         for s in range(slots):
-            rel = table[me, s] - row * columns
+            rel = table[s, me] - row * columns
             hit = (rel >= 0) & (rel < columns)
             slot = jnp.where(hit, s, slot)
             valid = jnp.where(hit, 1, valid)
@@ -197,7 +204,7 @@
     def inverse(c):
         def look(o, found):
             for s in range(slots):
-                found = jnp.where(table[o, s] == base + c, o, found)
+                found = jnp.where(table[s, o] == base + c, o, found)
             return found
 
         found = jnp.int32(n)
@@ -294,7 +301,7 @@
     bar[me] = bpk[me]
 
     def finish_ice(s):
-        block = table[me, s]
+        block = table[s, me]
         j = jnp.int32(0)
         for other in range(block_rows):
             rel = block - row_of(other) * columns
@@ -304,9 +311,6 @@
             io[s, f] = keep * st[j, f, pl.ds(PAD, BLK), :]
 
     loop(slots, finish_ice)
-    store_ice = pltpu.make_async_copy(io, ice_o, store_sem.at[0])
-    store_ice.start()
-
     @pl.when(me < n - 1)
     def _():
         halo(0, up).wait_send()
@@ -362,19 +366,10 @@
 
     loop(n, lambda d: wait_recv(cpk, car, cs, cr, d))
 
-    def store_early(c):
-        return pltpu.make_async_copy(acc.at[c, 0], ocean_o.at[0, :, :, lanes(c)], early_sem.at[c])
-
-    def store_late(c):
-        return pltpu.make_async_copy(
-            acc.at[c, 1:3], ocean_o.at[1:3, :, :, lanes(c)], late_sem.at[c]
-        )
-
     def heat(c):
         wet = 1.0 - land[base + c].astype(jnp.float32)
         cover = car[owner_of[c]]
         acc[c, 0, 0] += (TIME_STEP * HEAT_RATE * wet) * (cover * (FREEZING - oc[c, 0, 0]))
-        store_early(c).start()
 
     loop(columns, heat)
     loop(n, lambda d: wait_recv(bpk, bar, bs, br, d))
@@ -384,7 +379,6 @@
         o = owner_of[c]
         for f in range(2):
             acc[c, 1 + f, 0] += (TIME_STEP * STRESS_GAIN * wet) * bar[o, f]
-        store_late(c).start()
 
     loop(columns, stress)
 
@@ -394,9 +388,25 @@
         wait_send(bpk, bar, bs, br, d)
 
     loop(n, drain)
-    store_ice.wait()
-    loop(columns, lambda c: store_early(c).wait())
-    loop(columns, lambda c: store_late(c).wait())
+
+
+def settle(acc, io, ocean_o, ice_o, sems):
+    columns = acc.shape[0]
+    slots = io.shape[0]
+    store_ice = [
+        pltpu.make_async_copy(io.at[s], ice_o.at[s], sems.at[1 + s]) for s in range(slots)
+    ]
+    for copy in store_ice:
+        copy.start()
+
+    def store(c):
+        lanes = pl.ds(pl.multiple_of(c * BLK, BLK), BLK)
+        pltpu.make_async_copy(acc.at[c], ocean_o.at[:, :, :, lanes], sems.at[0]).start()
+
+    loop(columns, store)
+    pltpu.make_async_copy(acc, acc, sems.at[0]).wait()
+    for copy in store_ice:
+        copy.wait()
 
 
 def shards(n, ocean_state, ice_dynamics, ice_thickness, ice_table, land_mask):
@@ -405,20 +415,21 @@
     columns = width // BLK
     block_rows = n * rows // BLK
     f32 = jnp.float32
+    kept = 4 * (ocean_state.size + ice_dynamics.size) + 384 * 1024
     halo_rows = -(-3 * levels // 8) * 8
     dma = pltpu.SemaphoreType.DMA
-    smem = pl.BlockSpec(memory_space=pltpu.SMEM)
-    hbm = pl.BlockSpec(memory_space=pl.ANY)
-    return pl.pallas_call(
+    vmem = pl.BlockSpec(memory_space=pltpu.VMEM)
+    hbm = pl.BlockSpec(memory_space=pltpu.HBM)
+    anywhere = pl.BlockSpec(memory_space=pl.ANY)
+    ocean_next, ice_next = pl.pallas_call(
         functools.partial(kernel, n, columns, levels, slots, rows),
         out_shape=(
-            jax.ShapeDtypeStruct(ocean_state.shape, f32),
-            jax.ShapeDtypeStruct(ice_dynamics.shape, f32),
+            pltpu.VMEM((columns, 3, levels, rows, BLK), f32),
+            pltpu.VMEM(ice_dynamics.shape, f32),
         ),
-        in_specs=[smem, smem, hbm, hbm, hbm],
-        out_specs=(hbm, hbm),
+        in_specs=[hbm, hbm, hbm, hbm, hbm],
+        out_specs=(vmem, vmem),
         scratch_shapes=[
-            pltpu.VMEM((columns, 3, levels, rows, BLK), f32),
             pltpu.VMEM((columns, 3, levels, rows, BLK), f32),
             pltpu.VMEM(ice_dynamics.shape, f32),
             pltpu.VMEM(ice_thickness.shape, f32),
@@ -432,16 +443,28 @@
             pltpu.VMEM((n + 1, 2, rows, BLK), f32),
             pltpu.VMEM((block_rows, 5, BLK + 2 * PAD, BLK), f32),
             pltpu.VMEM((block_rows, 2, BLK, BLK), f32),
-            pltpu.VMEM(ice_dynamics.shape, f32),
             pltpu.SMEM((columns,), jnp.int32),
-            dma((2,)), dma((1,)), dma((columns,)), dma((columns,)), dma((columns,)),
+            pltpu.SMEM((slots, n), jnp.int32),
+            pltpu.SMEM(land_mask.shape, jnp.int32),
+            dma((5,)),
             dma((n,)), dma((n,)), dma((n,)), dma((n,)), dma((n,)), dma((n,)),
             dma((2,)), dma((2,)),
         ],
         compiler_params=pltpu.CompilerParams(
-            collective_id=0, has_side_effects=True, vmem_limit_bytes=48 * 1024 * 1024
+            collective_id=0, has_side_effects=True, vmem_limit_bytes=VMEM_BYTES - kept
         ),
-    )(ice_table, land_mask, ocean_state, ice_dynamics, ice_thickness)
+    )(ice_table.T, land_mask, ocean_state, ice_dynamics, ice_thickness)
+    return pl.pallas_call(
+        settle,
+        out_shape=(
+            jax.ShapeDtypeStruct(ocean_state.shape, f32),
+            jax.ShapeDtypeStruct(ice_dynamics.shape, f32),
+        ),
+        in_specs=[anywhere, anywhere],
+        out_specs=(hbm, hbm),
+        scratch_shapes=[dma((1 + slots,))],
+        compiler_params=pltpu.CompilerParams(vmem_limit_bytes=1024 * 1024),
+    )(ocean_next, ice_next)
 
 
 def solution(mesh):

time: 36.6 us -> 28.2 us (0.77)
  local copies, waits for them, and re-layouts: 7.04 us -> 0 us
  Pallas kernels: 28.6 us -> 27.4 us
    unnamed x11 -> x0, local copies, waits for them, and re-layouts: 7.04 us -> none
    pallas_call x1, Pallas kernels: 28.6 us -> 26 us  [shards(): pl.pallas_call(functools.partial(kernel, n, columns, levels, slots, rows)...]
    pallas_call x0 -> x1, Pallas kernels: none -> 1.39 us  [shards(): pl.pallas_call(settle, out_shape=(jax.ShapeDtypeStruct(ocean_state.shape,...]
where the time goes in v2:
time: 28.2 us; the launch traced here: 28 us
  Pallas kernels  27.4 us (97%)
  between operations  0.64 us (2%)
    pallas_call x1, Pallas kernels, shards(): pl.pallas_call(functools.partial(kernel, n, columns, levels, slots, rows)...  26 us
    pallas_call x1, Pallas kernels, shards(): pl.pallas_call(settle, out_shape=(jax.ShapeDtypeStruct(ocean_state.shape,...  1.39 us

profile of v2, /device:TPU:0, one launch (start us, length us, event | category | flops | bytes accessed | tf_op | source)
XLA Modules:
  0.0 28.0 jit_solution(9115867622405172938)
XLA Ops:
  0.6 26.0 %shard_map.68 = (f32[34,3,2,16,128]{4,3,2,1,0:T(8,128)S(1)}, f32[2,5,128,128]{3,2,1,0:T(8,128)S(1)}) custom-call(s32[2,16]{1,0:T(2,128)} %bitcast.1, s32[68]{0:T(128)} %land_h.1, f32[3,2,16,4352]{3,2,1,0:T(8,128)} %ocean_h.1, f32[2,5,128,128]{3,2,1,0:T(8,128)} %dyn_h.1, f32[2,5,128,128]{3,2,1,0:T(8,128)} %thick_h.1), custom_call_target="tpu_custom_call" | custom-call | tf_op jit(solution)/shard_map/pallas_call | solution.py:424
  26.6 1.4 %shard_map.69 = (f32[3,2,16,4352]{3,2,1,0:T(8,128)}, f32[2,5,128,128]{3,2,1,0:T(8,128)}) custom-call(f32[34,3,2,16,128]{4,3,2,1,0:T(8,128)S(1)} %get-tuple-element.4.acc, f32[2,5,128,128]{3,2,1,0:T(8,128)S(1)} %get-tuple-element.5.io), custom_call_target="tpu_custom_call" | custom-call | tf_op jit(solution)/shard_map/pallas_call | solution.py:457
